TPU v7x, 32 devices: a whole 2x2x4 slice. The times are simulated.
32 devices in a mesh: section: 2 (over core), dp: 4 (over y, x), expert: 4 (over z).
Axes of the slice: x: 2, y: 2, z: 4, core: 2. Of those that a mesh axis runs over, the one named last changes fastest.
Arguments:
- tokens: bfloat16 [2, 64, 2048], P('section', 'expert'), may hold values from -6 to 6
- out_grad: bfloat16 [2, 64, 2048], P('section', 'expert'), may hold values from -6 to 6
- expert_ids: int32 [2, 64, 8], P('section', 'expert'), may hold values from 0 to 63, all different within a row; in each aligned block of 16 rows (0 to 15, 16 to 31, ..., all dimensions but the last counted through in order) at most 3 rows name the same one
- gates: bfloat16 [2, 64, 8], P('section', 'expert'), may hold values from 0.049804688 to 0.59765625
- w_gate: bfloat16 [2, 64, 2048, 1024], P('section', 'expert', None, 'dp'), may hold values from -0.125 to 0.125
- w_up: bfloat16 [2, 64, 2048, 1024], P('section', 'expert', None, 'dp'), may hold values from -0.125 to 0.125
- w_down: bfloat16 [2, 64, 1024, 2048], P('section', 'expert', 'dp'), may hold values from -0.1875 to 0.1875
Outputs:
- prev_grad: bfloat16 [2, 64, 2048], P('section', 'expert', 'dp')
- gate_grad: float32 [2, 64, 8], P('section', 'expert', 'dp')
- grad_w_gate: bfloat16 [2, 64, 2048, 1024], P('section', 'expert', None, 'dp')
- grad_w_up: bfloat16 [2, 64, 2048, 1024], P('section', 'expert', None, 'dp')
- grad_w_down: bfloat16 [2, 64, 1024, 2048], P('section', 'expert', 'dp')
Inputs may be any that keep to these rules, and one draw needn't show every extreme that they name: `expert_ids`: each token names 8 different experts; within one section, the 16 tokens of one index of expert name any one expert at most 3 times.
All inputs are finite; a program needn't handle non-finite values.
Results may differ from a plain program's by a relative error of at most 0.0057.
Values may be sent and summed in bfloat16 or wider, within the bound.
A program may use at most 192 MiB of HBM per device.

v0:
```python
import jax
import jax.numpy as jnp
from jax import lax
from jax.sharding import PartitionSpec as P

CAP = 3


def from_behind(value, axis, steps):
    count = lax.axis_size(axis)
    pairs = [(source, (source + steps) % count) for source in range(count)]
    return lax.ppermute(value, axis, pairs)


def expert_backward(xs, dys, gs, wg, wu, wd):
    a = jnp.dot(xs, wg, preferred_element_type=jnp.float32)
    b = jnp.dot(xs, wu, preferred_element_type=jnp.float32)
    sig = jax.nn.sigmoid(a)
    silu = a * sig
    hid = silu * b
    dz = jnp.dot(dys, wd.T, preferred_element_type=jnp.float32)
    gate_f = gs.astype(jnp.float32)[:, None]
    dgate = jnp.sum(hid * dz, axis=1)
    dh = gate_f * dz
    db = (dh * silu).astype(jnp.bfloat16)
    da = (dh * b * sig * (1.0 + a * (1.0 - sig))).astype(jnp.bfloat16)
    hid_b = hid.astype(jnp.bfloat16)
    dout = (gate_f * dys.astype(jnp.float32)).astype(jnp.bfloat16)
    dwg = jnp.dot(xs.T, da, preferred_element_type=jnp.float32)
    dwu = jnp.dot(xs.T, db, preferred_element_type=jnp.float32)
    dwd = jnp.dot(hid_b.T, dout, preferred_element_type=jnp.float32)
    dxp = jnp.dot(da, wg.T, preferred_element_type=jnp.float32) + jnp.dot(
        db, wu.T, preferred_element_type=jnp.float32
    )
    return (dxp, dgate, dwg, dwu, dwd)


def local(tokens, out_grad, expert_ids, gates, w_gate, w_up, w_down):
    x_local = tokens[0]
    dy_local = out_grad[0]
    ids = expert_ids[0]
    tok_dev, top = ids.shape
    n_exp = lax.axis_size("expert")
    exp_loc = w_gate.shape[1]
    experts = exp_loc * n_exp
    slots = experts * CAP
    flat = ids.reshape(-1)
    onehot = (flat[:, None] == jnp.arange(experts, dtype=jnp.int32)[None, :]).astype(jnp.int32)
    rank = jnp.sum((jnp.cumsum(onehot, axis=0) - onehot) * onehot, axis=1)
    slot_of = flat * CAP + rank
    pair_map = (slot_of[:, None] == jnp.arange(slots, dtype=jnp.int32)[None, :]).astype(jnp.float32)
    token_map = jnp.sum(pair_map.reshape(tok_dev, top, slots), axis=1)
    token_map_b = token_map.astype(jnp.bfloat16)
    gate_slots = jnp.dot(
        gates[0].reshape(-1).astype(jnp.float32), pair_map, precision=lax.Precision.HIGHEST
    ).astype(jnp.bfloat16)
    x_slots = jnp.dot(token_map_b.T, x_local, preferred_element_type=jnp.float32).astype(
        jnp.bfloat16
    )
    dy_slots = jnp.dot(token_map_b.T, dy_local, preferred_element_type=jnp.float32).astype(
        jnp.bfloat16
    )
    recv_x, recv_dy, recv_gate = (
        lax.all_to_all(x_slots, "expert", split_axis=0, concat_axis=0, tiled=True),
        lax.all_to_all(dy_slots, "expert", split_axis=0, concat_axis=0, tiled=True),
        lax.all_to_all(gate_slots, "expert", split_axis=0, concat_axis=0, tiled=True),
    )

    def to_experts(arr):
        rest = arr.shape[1:]
        shaped = arr.reshape((n_exp, exp_loc, CAP) + rest)
        return jnp.swapaxes(shaped, 0, 1).reshape((exp_loc, n_exp * CAP) + rest)

    def from_experts(arr):
        rest = arr.shape[2:]
        shaped = arr.reshape((exp_loc, n_exp, CAP) + rest)
        return jnp.swapaxes(shaped, 0, 1).reshape((slots,) + rest)

    def per_expert(operands):
        return expert_backward(*operands)

    dxp, dgp, dwg, dwu, dwd = lax.map(
        per_expert,
        (
            to_experts(recv_x),
            to_experts(recv_dy),
            to_experts(recv_gate),
            w_gate[0],
            w_up[0],
            w_down[0],
        ),
    )
    dx_slot = from_experts(dxp)
    dg_slot = from_experts(dgp)
    back_dx, back_dg = (
        lax.all_to_all(dx_slot, "expert", split_axis=0, concat_axis=0, tiled=True),
        lax.all_to_all(dg_slot, "expert", split_axis=0, concat_axis=0, tiled=True),
    )
    dx_full = jnp.dot(token_map, back_dx, precision=lax.Precision.HIGHEST)
    dg_pairs = jnp.dot(pair_map, back_dg, precision=lax.Precision.HIGHEST).reshape(tok_dev, top)
    dx_token, dg_token = (
        lax.psum_scatter(dx_full, "dp", scatter_dimension=1, tiled=True),
        lax.psum_scatter(dg_pairs, "dp", scatter_dimension=1, tiled=True),
    )
    arrived = from_behind(dx_token.astype(jnp.bfloat16), "section", -1)
    return (
        arrived[None],
        dg_token[None],
        dwg.astype(jnp.bfloat16)[None],
        dwu.astype(jnp.bfloat16)[None],
        dwd.astype(jnp.bfloat16)[None],
    )


def solution(mesh):
    placed = (
        P("section", "expert", None),
        P("section", "expert", None),
        P("section", "expert", None),
        P("section", "expert", None),
        P("section", "expert", None, "dp"),
        P("section", "expert", None, "dp"),
        P("section", "expert", "dp", None),
    )
    return jax.shard_map(
        local,
        mesh=mesh,
        in_specs=placed,
        out_specs=(
            P("section", "expert", "dp"),
            P("section", "expert", "dp"),
            P("section", "expert", None, "dp"),
            P("section", "expert", None, "dp"),
            P("section", "expert", "dp", None),
        ),
        check_vma=False,
    )
```

profile of v0, /device:TPU:0, one launch (start us, length us, event | category | flops | bytes accessed | tf_op | source)
XLA Modules:
  0.0 392.6 jit_solution(13189627752245280733)
XLA Ops:
  10.3 6.3 %all-to-all-start = ((bf16[4,48,1]{1,2,0:T(2,128)(2,1)}), bf16[4,48,1]{1,2,0:T(2,128)(2,1)S(1)}, u32[]{:S(2)}, u32[]{:S(2)}) async-start(bf16[4,48,1]{1,2,0:T(2,128)(2,1)} %all_to_all.46), calls=%async_computation | async-start | bytes 4096 | tf_op jit(solution)/shard_map/all_to_all | solution.py:66
  18.9 3.1 all-to-all-done
  22.1 3.5 all-to-all-start.1
  25.6 2.1 convolution_convert_fusion
  27.7 16.8 %all-to-all-done.1 = bf16[4,48,2048]{2,1,0:T(8,128)(2,1)S(1)} async-done(((bf16[4,48,2048]{2,1,0:T(8,128)(2,1)}), bf16[4,48,2048]{2,1,0:T(8,128)(2,1)S(1)}, u32[]{:S(2)}, u32[]{:S(2)}) %all-to-all-start.1) | async-done | bytes 786464 | tf_op jit(solution)/shard_map/all_to_all | solution.py:65
  44.5 3.5 all-to-all-start.2
  49.9 17.6 %all-to-all-done.2 = bf16[4,48,2048]{2,1,0:T(8,128)(2,1)S(1)} async-done(((bf16[4,48,2048]{2,1,0:T(8,128)(2,1)}), bf16[4,48,2048]{2,1,0:T(8,128)(2,1)S(1)}, u32[]{:S(2)}, u32[]{:S(2)}) %all-to-all-start.2) | async-done | bytes 786464 | tf_op jit(solution)/shard_map/all_to_all | solution.py:64
  69.1 247.2 %while.18 = (s32[]{:T(128)}, f32[16,12,2048]{2,0,1:T(8,128)}, f32[16,12]{1,0:T(8,128)S(1)}, bf16[16,2048,256]{2,1,0:T(8,128)(2,1)}, bf16[16,2048,256]{2,1,0:T(8,...) while((s32[]{:T(128)}, f32[16,12,2048]{2,0,1:T(8,128)}, ...), condition=%wide.region_5.6_spmd, body=%wide.region_3.5_spmd.sunk | while | flops 100832256 | bytes 12755305 | solution.py:82
  72.0 1.7 multiply_reduce_fusion.2
  78.1 1.6 fusion.102
  79.7 1.6 fusion.103
  81.5 3.0 dynamic_update_slice.30
  87.5 1.7 multiply_reduce_fusion.2
  93.6 1.6 fusion.102
  95.2 1.6 fusion.103
  96.9 3.0 dynamic_update_slice.30
  103.0 1.7 multiply_reduce_fusion.2
  110.6 1.6 fusion.103
  112.4 3.0 dynamic_update_slice.30
  118.4 1.7 multiply_reduce_fusion.2
  126.1 1.6 fusion.103
  127.8 3.0 dynamic_update_slice.30
  133.9 1.7 multiply_reduce_fusion.2
  141.5 1.6 fusion.103
  143.3 3.0 dynamic_update_slice.30
  149.3 1.7 multiply_reduce_fusion.2
  157.0 1.6 fusion.103
  158.7 3.0 dynamic_update_slice.30
  164.8 1.7 multiply_reduce_fusion.2
  172.5 1.6 fusion.103
  174.2 3.0 dynamic_update_slice.30
  180.2 1.7 multiply_reduce_fusion.2
  187.9 1.6 fusion.103
  189.6 3.0 dynamic_update_slice.30
  195.7 1.7 multiply_reduce_fusion.2
  203.4 1.6 fusion.103
  205.1 3.0 dynamic_update_slice.30
  211.1 1.7 multiply_reduce_fusion.2
  218.8 1.6 fusion.103
  220.5 3.0 dynamic_update_slice.30
  226.6 1.7 multiply_reduce_fusion.2
  234.2 1.6 fusion.103
  236.0 3.0 dynamic_update_slice.30
  242.0 1.7 multiply_reduce_fusion.2
  249.7 1.6 fusion.103
  251.4 3.0 dynamic_update_slice.30
  257.4 1.7 multiply_reduce_fusion.2
  265.1 1.6 fusion.103
  266.9 3.0 dynamic_update_slice.30
  272.9 1.7 multiply_reduce_fusion.2
  280.6 1.6 fusion.103
  282.3 3.0 dynamic_update_slice.30
  288.3 1.7 multiply_reduce_fusion.2
  296.0 1.6 fusion.103
  297.8 3.0 dynamic_update_slice.30
  303.8 1.7 multiply_reduce_fusion.2
  311.5 1.6 fusion.103
  313.2 3.0 dynamic_update_slice.30
  316.3 2.5 copy.88
  319.6 39.0 %all_to_all.52 = f32[4,48,2048]{2,1,0:T(8,128)S(1)} all-to-all(f32[4,48,2048]{2,1,0:T(8,128)S(1)} %copy.89), channel_id=1, replica_groups=mesh['section'=2,'dp'=4,'expert'=4] {'expert'}, dimensions={0} | all-to-all | bytes 3145728 | tf_op jit(solution)/shard_map/all_to_all | solution.py:96
  361.0 3.2 all-to-all-start.4
  365.5 4.2 %all-to-all-done.4 = f32[4,48,1]{1,2,0:T(1,128)S(1)} async-done(((f32[4,48,1]{1,2,0:T(1,128)}), f32[4,48,1]{1,2,0:T(1,128)S(1)}, u32[]{:S(2)}, u32[]{:S(2)}) %all-to-all-start.4) | async-done | bytes 800 | tf_op jit(solution)/shard_map/all_to_all | solution.py:97
  371.6 9.9 %all-reduce = f32[16,8]{0,1:T(8,128)S(1)} all-reduce(f32[16,8]{0,1:T(8,128)S(1)} %bitcast.168), channel_id=3, replica_groups=mesh['section'=2,'dp'=4,'expert'=4] {'dp'}, use_global_device_ids=true, to_apply=%region_7.8.clone | all-reduce | flops 128 | bytes 1024
  381.5 1.7 reduce-scatter.2.cloned.1.call-done
  (200 shorter events, 158.8 us)
Async XLA Ops:
  7.2 10.5 %copy-start = (bf16[1,16,2048]{2,1,0:T(8,128)(2,1)S(1)}, bf16[1,16,2048]{2,1,0:T(8,128)(2,1)}, u32[]{:S(2)}) copy-start(bf16[1,16,2048]{2,1,0:T(8,128)(2,1)} %param.10) | copy-start | bytes 196612
  10.3 11.8 %all-to-all-start = ((bf16[4,48,1]{1,2,0:T(2,128)(2,1)}), bf16[4,48,1]{1,2,0:T(2,128)(2,1)S(1)}, u32[]{:S(2)}, u32[]{:S(2)}) async-start(bf16[4,48,1]{1,2,0:T(2,128)(2,1)} %all_to_all.46), calls=%async_computation | async-start | bytes 4096 | tf_op jit(solution)/shard_map/all_to_all | solution.py:66
  22.1 22.4 %all-to-all-start.1 = ((bf16[4,48,2048]{2,1,0:T(8,128)(2,1)}), bf16[4,48,2048]{2,1,0:T(8,128)(2,1)S(1)}, u32[]{:S(2)}, u32[]{:S(2)}) async-start(bf16[4,48,2048]{2,1,0:T(8,128)(2,1)} %bitcast.16), calls=%async_computation.1 | async-start | bytes 1572864 | tf_op jit(solution)/shard_map/all_to_all | solution.py:65
  44.5 23.1 %all-to-all-start.2 = ((bf16[4,48,2048]{2,1,0:T(8,128)(2,1)}), bf16[4,48,2048]{2,1,0:T(8,128)(2,1)S(1)}, u32[]{:S(2)}, u32[]{:S(2)}) async-start(bf16[4,48,2048]{2,1,0:T(8,128)(2,1)} %bitcast.22), calls=%async_computation.2 | async-start | bytes 1572864 | tf_op jit(solution)/shard_map/all_to_all | solution.py:64
  48.0 335.2 %reduce-scatter.2.cloned.1.call-start = ((), (), s32[]{:S(2)}) async-start(), calls=%async_computation.6 | async-start | bytes 163840 | tf_op jit(solution)/shard_map/reduce_scatter | solution.py:102
  69.1 295.2 %copy-start.2 = (u32[32]{0:T(128)S(1)}, u32[32]{0:T(128)}, u32[]{:S(2)}) copy-start(u32[32]{0:T(128)} %constant.51) | copy-start | bytes 388
  316.3 69.5 %copy-start.1 = (bf16[1,16,2048]{2,1,0:T(8,128)(2,1)S(1)}, bf16[1,16,2048]{2,1,0:T(8,128)(2,1)}, u32[]{:S(2)}) copy-start(bf16[1,16,2048]{2,1,0:T(8,128)(2,1)} %param.10) | copy-start | bytes 196612
  361.0 8.7 %all-to-all-start.4 = ((f32[4,48,1]{1,2,0:T(1,128)}), f32[4,48,1]{1,2,0:T(1,128)S(1)}, u32[]{:S(2)}, u32[]{:S(2)}) async-start(f32[4,48,1]{1,2,0:T(1,128)} %bitcast.35), calls=%async_computation.5 | async-start | bytes 4096 | tf_op jit(solution)/shard_map/all_to_all | solution.py:97
  383.9 1.2 collective-permute-start
Sparse Core Ops, SparseCore 0:
  360.2 22.8 reduce-scatter.1
where the time goes:
time: 397 us; the launch traced here: 393 us
  matrix products  202 us (51%)
  local copies, waits for them, and re-layouts  63.3 us (16%)
  blocking collectives  48.9 us (12%)
  waiting for transfers between devices  44 us (11%)
  starting transfers between devices  16.6 us (4%)
  between operations  14.9 us (4%)
    dynamic_update_slice x48, local copies, waits for them, and re-layouts, local(): lax.map(per_expert, (to_experts(recv_x), to_experts(recv_dy), to_experts(...  50.7 us
    all_to_all x1, blocking collectives, local(): lax.all_to_all(dx_slot, 'expert', split_axis=0, concat_axis=0, tiled=True)  39 us
    dot_general x16, matrix products, expert_backward(): dz = jnp.dot(dys, wd.T, preferred_element_type=jnp.float32)  27.7 us
    dot_general x16, matrix products, expert_backward(): jnp.dot(db, wu.T, preferred_element_type=jnp.float32)  25.8 us
    dot_general x16, matrix products, expert_backward(): jnp.dot(da, wg.T, preferred_element_type=jnp.float32)  25.5 us
    dot_general x16, matrix products, expert_backward(): b = jnp.dot(xs, wu, preferred_element_type=jnp.float32)  23.6 us
    dot_general x16, matrix products, expert_backward(): a = jnp.dot(xs, wg, preferred_element_type=jnp.float32)  23.6 us
    dot_general x16, matrix products, expert_backward(): dwg = jnp.dot(xs.T, da, preferred_element_type=jnp.float32)  23.4 us
  transfers between devices with their start and end apart: 6, of which 6 were waited for; matrix products, arithmetic and copies ran while one was open for 2% of the time, Pallas kernels for 0%

commit v1 on v0

v1 whole, which is shorter than its diff:
```python
import functools

import jax
import jax.numpy as jnp
from jax import lax
from jax.experimental import pallas as pl
from jax.experimental.pallas import tpu as pltpu
from jax.sharding import PartitionSpec as P

BF = jnp.bfloat16
F32 = jnp.float32
MESH = pl.DeviceIdType.MESH
VMEM = pl.BlockSpec(memory_space=pltpu.VMEM)
LIMIT = 60 * 1024 * 1024


def each(start, stop, body):
    if stop - start <= 8:
        for i in range(start, stop):
            body(i)
    else:
        lax.fori_loop(start, stop, lambda i, c: (body(i), c)[1], 0)


def signal(barrier, where):
    pl.semaphore_signal(barrier, inc=1, device_id=where, device_id_type=MESH)


def push(src, dst, send, recv, where):
    return pltpu.make_async_remote_copy(
        src_ref=src, dst_ref=dst, send_sem=send, recv_sem=recv, device_id=where, device_id_type=MESH
    )


def gather_kernel(n, ndp, x_ref, dy_ref, ids_ref, gates_ref, xy_ref, g_ref, s1, r1, sg, rg, s2, r2):
    me = lax.axis_index("expert")
    d = lax.axis_index("dp")
    rows, width = x_ref.shape
    top = ids_ref.shape[1]
    lanes = g_ref.shape[2]
    part = width // ndp
    barrier = pltpu.get_barrier_semaphore()
    each(1, n, lambda o: signal(barrier, {"expert": lax.rem(me + o, n)}))
    each(1, ndp, lambda o: signal(barrier, {"dp": lax.rem(d + o, ndp)}))

    mine = pl.ds(pl.multiple_of(me * rows, rows), rows)
    xy_ref[0, mine, :] = x_ref[...]
    xy_ref[1, mine, :] = dy_ref[...]
    lane = lax.broadcasted_iota(jnp.int32, (rows, lanes), 1)
    ids = ids_ref[...]
    gates = gates_ref[...].astype(F32)
    g = jnp.zeros((rows, lanes), F32)
    for k in range(top):
        g = g + jnp.where(lane == ids[:, k : k + 1], gates[:, k : k + 1], 0.0)
    g_ref[me] = g
    pl.semaphore_wait(barrier, n - 1 + ndp - 1)

    cols = pl.ds(pl.multiple_of(d * part, 128), part)

    def block(e):
        return xy_ref.at[:, pl.ds(pl.multiple_of(e * rows, rows), rows), cols]

    def along(o):
        to = {"expert": lax.rem(me + o, n)}
        return push(block(me), block(me), s1.at[o], r1.at[o], to)

    def gate(o):
        to = {"expert": lax.rem(me + o, n)}
        return push(g_ref.at[me], g_ref.at[me], sg.at[o], rg.at[o], to)

    def spread(o, q):
        e = lax.rem(me - o + n, n)
        to = {"dp": lax.rem(d + q, ndp)}
        return push(block(e), block(e), s2.at[o, q], r2.at[o, q], to)

    each(1, n, lambda o: along(o).start())
    each(1, n, lambda o: gate(o).start())

    def pass_on(o):
        along(o).wait_recv()
        each(1, ndp, lambda q: spread(o, q).start())

    each(1, n, pass_on)

    def finish(o):
        along(o).wait_send()
        gate(o).wait()
        each(1, ndp, lambda q: spread(o, q).wait())

    each(1, n, finish)


def gather(x, dy, ids, gates, n, ndp, lanes):
    rows, width = x.shape
    dma = pltpu.SemaphoreType.DMA
    return pl.pallas_call(
        functools.partial(gather_kernel, n, ndp),
        out_shape=(
            jax.ShapeDtypeStruct((2, n * rows, width), BF),
            jax.ShapeDtypeStruct((n, rows, lanes), F32),
        ),
        in_specs=[VMEM] * 4,
        out_specs=(VMEM, VMEM),
        scratch_shapes=[dma((n,)), dma((n,)), dma((n,)), dma((n,)), dma((n, ndp)), dma((n, ndp))],
        compiler_params=pltpu.CompilerParams(
            collective_id=0, has_side_effects=True, vmem_limit_bytes=LIMIT
        ),
        name="gather_tokens",
    )(x, dy, ids, gates)


def nt(a, b):
    return lax.dot_general(a, b, (((1,), (1,)), ((), ())), preferred_element_type=F32)


def nn(a, b):
    return jnp.dot(a, b, preferred_element_type=F32)


def expert_kernel(
    base_ref, xy_ref, g_ref, wg_ref, wu_ref, wd_ref, dx_ref, dg_ref, ogate, oup, odown, xt, acc, dgs
):
    e = pl.program_id(0)
    last = pl.num_programs(0) - 1
    tok = xy_ref.shape[1]
    width = xy_ref.shape[2]
    chunk = 256

    @pl.when(e == 0)
    def _():
        def turn(i, c):
            at = pl.ds(pl.multiple_of(i * chunk, chunk), chunk)
            xt[at, :] = xy_ref[0, :, at].T
            return c

        lax.fori_loop(0, width // chunk, turn, 0)
        acc[...] = jnp.zeros_like(acc)
        dgs[...] = jnp.zeros_like(dgs)

    lane = lax.broadcasted_iota(jnp.int32, g_ref.shape, 1)
    here = lane == e + base_ref[0]
    g = jnp.sum(jnp.where(here, g_ref[...], 0.0), axis=1, keepdims=True)
    x = xy_ref[0]
    dy = xy_ref[1]
    a = nn(x, wg_ref[0])
    b = nn(x, wu_ref[0])
    dz = nt(dy, wd_ref[0])
    sig = jax.nn.sigmoid(a)
    silu = a * sig
    hid = silu * b
    dgs[...] += jnp.where(here, jnp.sum(hid * dz, axis=1, keepdims=True), 0.0)
    dh = g * dz
    db = (dh * silu).astype(BF)
    da = (dh * b * sig * (1.0 + a * (1.0 - sig))).astype(BF)
    hid_t = hid.astype(BF).T

    for i in range(width // chunk):
        at = slice(i * chunk, (i + 1) * chunk)
        acc[:, at] += nt(da, wg_ref[0, at, :]) + nt(db, wu_ref[0, at, :])
        xc = xt[at, :]
        ogate[0, at, :] = nn(xc, da).astype(BF)
        oup[0, at, :] = nn(xc, db).astype(BF)
        dout = (g * xy_ref[1, :, at].astype(F32)).astype(BF)
        odown[0, :, at] = nn(hid_t, dout).astype(BF)

    @pl.when(e == last)
    def _():
        dx_ref[...] = acc[...].astype(BF)
        dg_ref[...] = dgs[...]


def experts(base, xy, g, wg, wu, wd):
    count, width, hidden = wg.shape
    tok = xy.shape[1]
    lanes = g.shape[1]
    whole = lambda *shape: pl.BlockSpec(shape, lambda e, b: (0,) * len(shape))
    one = lambda *shape: pl.BlockSpec((1,) + shape, lambda e, b: (e, 0, 0))
    return pl.pallas_call(
        expert_kernel,
        grid_spec=pltpu.PrefetchScalarGridSpec(
            num_scalar_prefetch=1,
            grid=(count,),
            in_specs=[
                whole(2, tok, width),
                whole(tok, lanes),
                one(width, hidden),
                one(width, hidden),
                one(hidden, width),
            ],
            out_specs=[
                whole(tok, width),
                whole(tok, lanes),
                one(width, hidden),
                one(width, hidden),
                one(hidden, width),
            ],
            scratch_shapes=[
                pltpu.VMEM((width, tok), BF),
                pltpu.VMEM((tok, width), F32),
                pltpu.VMEM((tok, lanes), F32),
            ],
        ),
        out_shape=(
            jax.ShapeDtypeStruct((tok, width), BF),
            jax.ShapeDtypeStruct((tok, lanes), F32),
            jax.ShapeDtypeStruct(wg.shape, BF),
            jax.ShapeDtypeStruct(wu.shape, BF),
            jax.ShapeDtypeStruct(wd.shape, BF),
        ),
        compiler_params=pltpu.CompilerParams(vmem_limit_bytes=LIMIT),
        name="experts",
    )(base, xy, g, wg, wu, wd)


def reduce_kernel(
    n, ndp, dx_ref, dg_ref, ids_ref, out_ref, gg_ref,
    rb, gb, sb, hb, rb2, gb2, s1, r1, sg, rg, s2, r2, sh, rh
):
    me = lax.axis_index("expert")
    d = lax.axis_index("dp")
    sec = lax.axis_index("section")
    nsec = lax.axis_size("section")
    to_sec = lax.rem(sec + nsec - 1, nsec)
    rows, part = out_ref.shape
    lanes = dg_ref.shape[1]
    barrier = pltpu.get_barrier_semaphore()
    each(1, ndp, lambda o: signal(barrier, {"dp": lax.rem(d + o, ndp)}))
    each(1, n, lambda o: signal(barrier, {"expert": lax.rem(me + o, n)}))
    each(0, n, lambda o: signal(barrier, {"section": to_sec, "expert": lax.rem(me + o, n)}))
    pl.semaphore_wait(barrier, ndp - 1 + n - 1 + n)

    def cols(p):
        return pl.ds(pl.multiple_of(p * part, 128), part)

    def first(o):
        p = lax.rem(d + o, ndp)
        return push(dx_ref.at[:, cols(p)], rb.at[o], s1.at[o], r1.at[o], {"dp": p})

    def first_g(o):
        p = lax.rem(d + o, ndp)
        return push(dg_ref, gb.at[o], sg.at[o], rg.at[o], {"dp": p})

    each(1, ndp, lambda o: first(o).start())
    each(1, ndp, lambda o: first_g(o).start())

    def wait_first(o):
        first_g(o).wait()
        first(o).wait()

    each(1, ndp, wait_first)

    def sums(e):
        at = pl.ds(pl.multiple_of(e * rows, rows), rows)
        t = dx_ref[at, cols(d)].astype(F32)
        u = dg_ref[at, :]
        for o in range(1, ndp):
            t = t + rb[o, at, :].astype(F32)
            u = u + gb[o, at, :]
        sb[e] = t
        hb[e] = u

    each(0, n, sums)

    def second(o):
        p = lax.rem(me + o, n)
        return push(sb.at[p], rb2.at[o], s2.at[o], r2.at[o], {"section": to_sec, "expert": p})

    def second_g(o):
        p = lax.rem(me + o, n)
        return push(hb.at[p], gb2.at[o], sh.at[o], rh.at[o], {"expert": p})

    each(0, n, lambda o: second(o).start())
    each(1, n, lambda o: second_g(o).start())
    each(1, n, lambda o: second_g(o).wait())
    each(0, n, lambda o: second(o).wait())
    out_ref[...] = jnp.sum(rb2[...], axis=0)

    if n <= 8:
        u = hb[me]
        for o in range(1, n):
            u = u + gb2[o]
    else:
        u = lax.fori_loop(1, n, lambda o, u: u + gb2[o], hb[me])
    ids = ids_ref[...]
    top = ids.shape[1]
    mine = gg_ref.shape[1]
    lane = lax.broadcasted_iota(jnp.int32, (rows, lanes), 1)
    spot = lax.broadcasted_iota(jnp.int32, (rows, mine), 1)
    res = jnp.zeros((rows, mine), F32)
    for k in range(top):
        v = jnp.sum(jnp.where(lane == ids[:, k : k + 1], u, 0.0), axis=1, keepdims=True)
        res = res + jnp.where(spot + d * mine == k, v, 0.0)
    gg_ref[...] = res


def reduce(dx, dg, ids, n, ndp):
    tok, width = dx.shape
    lanes = dg.shape[1]
    rows = tok // n
    part = width // ndp
    top = ids.shape[1]
    dma = pltpu.SemaphoreType.DMA
    return pl.pallas_call(
        functools.partial(reduce_kernel, n, ndp),
        out_shape=(
            jax.ShapeDtypeStruct((rows, part), F32),
            jax.ShapeDtypeStruct((rows, top // ndp), F32),
        ),
        in_specs=[VMEM] * 3,
        out_specs=(VMEM, VMEM),
        scratch_shapes=[
            pltpu.VMEM((ndp, tok, part), BF),
            pltpu.VMEM((ndp, tok, lanes), F32),
            pltpu.VMEM((n, rows, part), F32),
            pltpu.VMEM((n, rows, lanes), F32),
            pltpu.VMEM((n, rows, part), F32),
            pltpu.VMEM((n, rows, lanes), F32),
            dma((ndp,)), dma((ndp,)), dma((ndp,)), dma((ndp,)),
            dma((n,)), dma((n,)), dma((n,)), dma((n,)),
        ],
        compiler_params=pltpu.CompilerParams(
            collective_id=1, has_side_effects=True, vmem_limit_bytes=LIMIT
        ),
        name="reduce_dx",
    )(dx, dg, ids)


def local(tokens, out_grad, expert_ids, gates, w_gate, w_up, w_down):
    n = lax.axis_size("expert")
    ndp = lax.axis_size("dp")
    exp_loc = w_gate.shape[1]
    lanes = -(-exp_loc * n // 128) * 128
    xy, g = gather(tokens[0], out_grad[0], expert_ids[0], gates[0], n, ndp, lanes)
    base = (lax.axis_index("expert") * exp_loc).astype(jnp.int32).reshape(1)
    dx, dg, dwg, dwu, dwd = experts(
        base, xy, g.reshape(-1, lanes), w_gate[0], w_up[0], w_down[0]
    )
    prev, gg = reduce(dx, dg, expert_ids[0], n, ndp)
    return prev.astype(BF)[None], gg[None], dwg[None], dwu[None], dwd[None]


def solution(mesh):
    placed = (
        P("section", "expert", None),
        P("section", "expert", None),
        P("section", "expert", None),
        P("section", "expert", None),
        P("section", "expert", None, "dp"),
        P("section", "expert", None, "dp"),
        P("section", "expert", "dp", None),
    )
    return jax.shard_map(
        local,
        mesh=mesh,
        in_specs=placed,
        out_specs=(
            P("section", "expert", "dp"),
            P("section", "expert", "dp"),
            P("section", "expert", None, "dp"),
            P("section", "expert", None, "dp"),
            P("section", "expert", "dp", None),
        ),
        check_vma=False,
    )
```

time: 397 us -> 87.8 us (0.22); the launches traced: 393 us -> 87.4 us
  matrix products: 202 us -> 0 us
  Pallas kernels: 0 us -> 81.4 us
  local copies, waits for them, and re-layouts: 63.3 us -> 4.03 us
  blocking collectives: 48.9 us -> 0 us
  waiting for transfers between devices: 44 us -> 0 us
  starting transfers between devices: 16.6 us -> 0 us
  between operations: 14.9 us -> 0.65 us
    dot_general x133 -> x0, matrix products: 202 us -> none  [the longest x16 27.7 us: expert_backward(): dz = jnp.dot(dys, wd.T, preferred_element_type=jnp.float32)]
    pallas_call x0 -> x3, Pallas kernels: none -> 81.4 us  [the longest x1 49.5 us: experts(): pl.pallas_call(expert_kernel, grid_spec=pltpu.PrefetchScalarGridSpec(num_...]
    dynamic_update_slice x48 -> x0, local copies, waits for them, and re-layouts: 50.7 us -> none  [local(): lax.map(per_expert, (to_experts(recv_x), to_experts(recv_dy), to_experts(...]
    all_to_all x4 -> x0, waiting for transfers between devices: 41.7 us -> none  [the longest x1 17.6 us: local(): lax.all_to_all(x_slots, 'expert', split_axis=0, concat_axis=0, tiled=True)]
    all_to_all x1 -> x0, blocking collectives: 39 us -> none  [local(): lax.all_to_all(dx_slot, 'expert', split_axis=0, concat_axis=0, tiled=True)]
    all_to_all x4 -> x0, starting transfers between devices: 16.5 us -> none  [the longest x1 6.32 us: local(): lax.all_to_all(gate_slots, 'expert', split_axis=0, concat_axis=0, tiled=T...]
    unnamed x1 -> x0, blocking collectives: 9.88 us -> none
    all_to_all x7 -> x0, local copies, waits for them, and re-layouts: 4.09 us -> none  [the longest x3 1.27 us: local(): lax.all_to_all(dg_slot, 'expert', split_axis=0, concat_axis=0, tiled=True)]
  transfers between devices with their start and end apart: 6 -> 0, of which waited for: 6 -> 0; matrix products, arithmetic and copies ran while one was open for 2% -> 0% of each run, Pallas kernels for 0% -> 0%
where the time goes in v1:
time: 87.8 us; the launch traced here: 87.4 us
  Pallas kernels  81.4 us (93%)
  local copies, waits for them, and re-layouts  4.03 us (5%)
  other arithmetic  1.37 us (2%)
    pallas_call x1, Pallas kernels, experts(): pl.pallas_call(expert_kernel, grid_spec=pltpu.PrefetchScalarGridSpec(num_...  49.5 us
    pallas_call x1, Pallas kernels, gather(): pl.pallas_call(functools.partial(gather_kernel, n, ndp), out_shape=(jax.S...  16 us
    pallas_call x1, Pallas kernels, reduce(): pl.pallas_call(functools.partial(reduce_kernel, n, ndp), out_shape=(jax.S...  15.9 us

profile of v1, /device:TPU:0, one launch (start us, length us, event | category | flops | bytes accessed | tf_op | source)
XLA Modules:
  0.0 87.4 jit_solution(2591000310294548515)
XLA Ops:
  0.6 1.3 %copy.13.gates_ref = bf16[16,8]{1,0:T(8,128)(2,1)} copy(bf16[16,8]{0,1:T(8,128)(2,1)} %bitcast.22) | data formatting | bytes 512 | tf_op jit(solution)/shard_map/squeeze | solution.py:333
  2.0 1.4 %copy.12.ids_ref = s32[16,8]{1,0:T(8,128)} copy(s32[16,8]{0,1:T(8,128)} %bitcast.21) | data formatting | bytes 1024 | tf_op jit(solution)/shard_map/squeeze | solution.py:333
  3.3 16.0 %gather_tokens.1 = (bf16[2,64,2048]{2,1,0:T(8,128)(2,1)}, f32[4,16,128]{2,1,0:T(8,128)}) custom-call(bf16[16,2048]{1,0:T(8,128)(2,1)} %bitcast.18, bf16[16,2048]{1,0:T(8,128)(2,1)} %bitcast.19, s32[16,8]{1,0:T(8,128)} %copy.12.ids_ref, bf16[16,8]{1,0:T(8,128)(2,1)} %copy.13.gates_ref), custom_call_target="tpu_custom_call" | custom-call | tf_op jit(solution)/shard_map/gather_tokens/pallas_call | solution.py:96
  19.3 49.5 %experts.1 = (bf16[64,2048]{1,0:T(8,128)(2,1)}, f32[64,128]{1,0:T(8,128)}, bf16[16,2048,256]{2,1,0:T(8,128)(2,1)}, bf16[16,2048,256]{2,1,0:T(8,128)(2,1)}, bf16[16,256,2048]{2,1,0:T(8,128)(2,1)}) custom-call(s32[1]{0:T(128)} %bitcast.base_ref, bf16[2,64,2048]{2,1,0:T(8,128)(2,1)} %get-tuple-element.14.xy_ref, f32[64,128]{1,0:T(8,128)} %bitcast.20, ...), custom_call_target="tpu_custom_call" | custom-call | tf_op jit(solution)/shard_map/experts/pallas_call | solution.py:178
  68.8 15.9 %reduce_dx.1 = (f32[16,512]{1,0:T(8,128)}, f32[16,2]{1,0:T(8,128)}) custom-call(bf16[64,2048]{1,0:T(8,128)(2,1)} %get-tuple-element.16.dx_ref, f32[64,128]{1,0:T(8,128)} %get-tuple-element.17.dg_ref, s32[16,8]{1,0:T(8,128)} %copy.12.ids_ref), custom_call_target="tpu_custom_call" | custom-call | tf_op jit(solution)/shard_map/reduce_dx/pallas_call | solution.py:303
  84.7 1.4 %convert_bitcast_fusion = bf16[1,16,512]{2,1,0:T(8,128)(2,1)} fusion(f32[16,512]{1,0:T(8,128)} %get-tuple-element.18), kind=kLoop, calls=%fused_computation | loop fusion | flops 8192 | bytes 49152 | tf_op jit(solution)/shard_map/broadcast_in_dim | solution.py:339
  86.1 1.3 %copy.15 = f32[16,2]{0,1:T(2,128)} copy(f32[16,2]{1,0:T(8,128)} %get-tuple-element.19) | data formatting | bytes 256 | tf_op jit(solution)/shard_map/reduce_dx/pallas_call | solution.py:303

commit v2 on v1

--- a/solution.py
+++ b/solution.py
@@ -32,11 +32,22 @@
     )
 
 
+def columns_of(ref):
+    v = ref[...].astype(F32)
+    top = v.shape[0]
+    one = lax.broadcasted_iota(jnp.int32, (top, top), 0)
+    two = lax.broadcasted_iota(jnp.int32, (top, top), 1)
+    eye = jnp.where(one == two, 1.0, 0.0)
+    return lax.dot_general(
+        v, eye, (((0,), (0,)), ((), ())), precision=lax.Precision.HIGHEST, preferred_element_type=F32
+    )
+
+
 def gather_kernel(n, ndp, x_ref, dy_ref, ids_ref, gates_ref, xy_ref, g_ref, s1, r1, sg, rg, s2, r2):
     me = lax.axis_index("expert")
     d = lax.axis_index("dp")
     rows, width = x_ref.shape
-    top = ids_ref.shape[1]
+    top = ids_ref.shape[0]
     lanes = g_ref.shape[2]
     part = width // ndp
     barrier = pltpu.get_barrier_semaphore()
@@ -46,9 +57,9 @@
     mine = pl.ds(pl.multiple_of(me * rows, rows), rows)
     xy_ref[0, mine, :] = x_ref[...]
     xy_ref[1, mine, :] = dy_ref[...]
-    lane = lax.broadcasted_iota(jnp.int32, (rows, lanes), 1)
-    ids = ids_ref[...]
-    gates = gates_ref[...].astype(F32)
+    lane = lax.broadcasted_iota(jnp.int32, (rows, lanes), 1).astype(F32)
+    ids = columns_of(ids_ref)
+    gates = columns_of(gates_ref)
     g = jnp.zeros((rows, lanes), F32)
     for k in range(top):
         g = g + jnp.where(lane == ids[:, k : k + 1], gates[:, k : k + 1], 0.0)
@@ -118,88 +129,140 @@
 
 
 def expert_kernel(
-    base_ref, xy_ref, g_ref, wg_ref, wu_ref, wd_ref, dx_ref, dg_ref, ogate, oup, odown, xt, acc, dgs
+    nin, nout, base_ref, xy_ref, g_ref, wg_ref, wu_ref, wd_ref, dx_ref, dg_ref, ogate, oup, odown,
+    xt, acc, sda, sdb, sht, sg, bg, bu, bd, cg, cu, cd, sin, sout
 ):
-    e = pl.program_id(0)
-    last = pl.num_programs(0) - 1
-    tok = xy_ref.shape[1]
-    width = xy_ref.shape[2]
+    count, width, hidden = wg_ref.shape
     chunk = 256
 
-    @pl.when(e == 0)
-    def _():
-        def turn(i, c):
-            at = pl.ds(pl.multiple_of(i * chunk, chunk), chunk)
-            xt[at, :] = xy_ref[0, :, at].T
-            return c
-
-        lax.fori_loop(0, width // chunk, turn, 0)
-        acc[...] = jnp.zeros_like(acc)
-        dgs[...] = jnp.zeros_like(dgs)
-
+    def load(e):
+        slot = lax.rem(e, nin)
+        pairs = ((wg_ref, bg), (wu_ref, bu), (wd_ref, bd))
+        return [
+            pltpu.make_async_copy(src.at[e], dst.at[slot], sin.at[i, slot])
+            for i, (src, dst) in enumerate(pairs)
+        ]
+
+    def store(e):
+        slot = lax.rem(e, nout)
+        pairs = ((cg, ogate), (cu, oup), (cd, odown))
+        return [
+            pltpu.make_async_copy(src.at[slot], dst.at[e], sout.at[i, slot])
+            for i, (src, dst) in enumerate(pairs)
+        ]
+
+    for e in range(nin):
+        for c in load(e):
+            c.start()
+
+    def turn(i, c):
+        at = pl.ds(pl.multiple_of(i * chunk, chunk), chunk)
+        xt[at, :] = xy_ref[0, :, at].T
+        return c
+
+    lax.fori_loop(0, width // chunk, turn, 0)
+    acc[...] = jnp.zeros_like(acc)
+    dg_ref[...] = jnp.zeros_like(dg_ref)
     lane = lax.broadcasted_iota(jnp.int32, g_ref.shape, 1)
-    here = lane == e + base_ref[0]
-    g = jnp.sum(jnp.where(here, g_ref[...], 0.0), axis=1, keepdims=True)
-    x = xy_ref[0]
-    dy = xy_ref[1]
-    a = nn(x, wg_ref[0])
-    b = nn(x, wu_ref[0])
-    dz = nt(dy, wd_ref[0])
-    sig = jax.nn.sigmoid(a)
-    silu = a * sig
-    hid = silu * b
-    dgs[...] += jnp.where(here, jnp.sum(hid * dz, axis=1, keepdims=True), 0.0)
-    dh = g * dz
-    db = (dh * silu).astype(BF)
-    da = (dh * b * sig * (1.0 + a * (1.0 - sig))).astype(BF)
-    hid_t = hid.astype(BF).T
-
-    for i in range(width // chunk):
-        at = slice(i * chunk, (i + 1) * chunk)
-        acc[:, at] += nt(da, wg_ref[0, at, :]) + nt(db, wu_ref[0, at, :])
-        xc = xt[at, :]
-        ogate[0, at, :] = nn(xc, da).astype(BF)
-        oup[0, at, :] = nn(xc, db).astype(BF)
-        dout = (g * xy_ref[1, :, at].astype(F32)).astype(BF)
-        odown[0, :, at] = nn(hid_t, dout).astype(BF)
-
-    @pl.when(e == last)
-    def _():
-        dx_ref[...] = acc[...].astype(BF)
-        dg_ref[...] = dgs[...]
-
-
-def experts(base, xy, g, wg, wu, wd):
+
+    def forward(e):
+        for c in load(e):
+            c.wait()
+        k = lax.rem(e, nin)
+        here = lane == e + base_ref[0]
+        g = jnp.sum(jnp.where(here, g_ref[...], 0.0), axis=1, keepdims=True)
+        a = nn(xy_ref[0], bg[k])
+        b = nn(xy_ref[0], bu[k])
+        dz = nt(xy_ref[1], bd[k])
+        return here, g, a, b, dz
+
+    def middle(here, g, a, b, dz):
+        sig = jax.nn.sigmoid(a)
+        silu = a * sig
+        hid = silu * b
+        dg_ref[...] += jnp.where(here, jnp.sum(hid * dz, axis=1, keepdims=True), 0.0)
+        dh = g * dz
+        sdb[...] = (dh * silu).astype(BF)
+        sda[...] = (dh * b * sig * (1.0 + a * (1.0 - sig))).astype(BF)
+        sht[...] = hid.astype(BF).T
+        sg[...] = jnp.broadcast_to(g, sg.shape)
+
+    def held():
+        return sda[...], sdb[...], sht[...], sg[:, :1]
+
+    def backward(e, da, db, hid_t, g):
+        k = lax.rem(e, nin)
+        o = lax.rem(e, nout)
+        for i in range(width // chunk):
+            at = slice(i * chunk, (i + 1) * chunk)
+            xc = xt[at, :]
+            acc[:, at] += nt(da, bg[k, at, :]) + nt(db, bu[k, at, :])
+            cg[o, at, :] = nn(xc, da).astype(BF)
+            cu[o, at, :] = nn(xc, db).astype(BF)
+            dout = (g * xy_ref[1, :, at].astype(F32)).astype(BF)
+            cd[o, :, at] = nn(hid_t, dout).astype(BF)
+
+    def free(e):
+        @pl.when(e >= nout)
+        def _():
+            for c in store(e - nout):
+                c.wait()
+
+    def expert(e, carry):
+        free(e)
+        old = held()
+        new = forward(e + 1)
+        backward(e, *old)
+        middle(*new)
+        for c in store(e):
+            c.start()
+
+        @pl.when(e + nin < count)
+        def _():
+            for c in load(e + nin):
+                c.start()
+
+        return carry
+
+    middle(*forward(0))
+    lax.fori_loop(0, count - 1, expert, 0)
+    free(count - 1)
+    backward(count - 1, *held())
+    for c in store(count - 1):
+        c.start()
+    dx_ref[...] = acc[...].astype(BF)
+    for e in range(count - nout, count):
+        for c in store(e):
+            c.wait()
+
+
+def experts(base, xy, g, wg, wu, wd, nin=4, nout=3):
     count, width, hidden = wg.shape
     tok = xy.shape[1]
     lanes = g.shape[1]
-    whole = lambda *shape: pl.BlockSpec(shape, lambda e, b: (0,) * len(shape))
-    one = lambda *shape: pl.BlockSpec((1,) + shape, lambda e, b: (e, 0, 0))
+    nin, nout = min(nin, count), min(nout, count)
+    hbm = pl.BlockSpec(memory_space=pl.ANY)
+    dma = pltpu.SemaphoreType.DMA
     return pl.pallas_call(
-        expert_kernel,
-        grid_spec=pltpu.PrefetchScalarGridSpec(
-            num_scalar_prefetch=1,
-            grid=(count,),
-            in_specs=[
-                whole(2, tok, width),
-                whole(tok, lanes),
-                one(width, hidden),
-                one(width, hidden),
-                one(hidden, width),
-            ],
-            out_specs=[
-                whole(tok, width),
-                whole(tok, lanes),
-                one(width, hidden),
-                one(width, hidden),
-                one(hidden, width),
-            ],
-            scratch_shapes=[
-                pltpu.VMEM((width, tok), BF),
-                pltpu.VMEM((tok, width), F32),
-                pltpu.VMEM((tok, lanes), F32),
-            ],
-        ),
+        functools.partial(expert_kernel, nin, nout),
+        in_specs=[pl.BlockSpec(memory_space=pltpu.SMEM), VMEM, VMEM, hbm, hbm, hbm],
+        out_specs=(VMEM, VMEM, hbm, hbm, hbm),
+        scratch_shapes=[
+            pltpu.VMEM((width, tok), BF),
+            pltpu.VMEM((tok, width), F32),
+            pltpu.VMEM((tok, hidden), BF),
+            pltpu.VMEM((tok, hidden), BF),
+            pltpu.VMEM((hidden, tok), BF),
+            pltpu.VMEM((tok, 128), F32),
+            pltpu.VMEM((nin, width, hidden), BF),
+            pltpu.VMEM((nin, width, hidden), BF),
+            pltpu.VMEM((nin, hidden, width), BF),
+            pltpu.VMEM((nout, width, hidden), BF),
+            pltpu.VMEM((nout, width, hidden), BF),
+            pltpu.VMEM((nout, hidden, width), BF),
+            dma((3, nin)),
+            dma((3, nout)),
+        ],
         out_shape=(
             jax.ShapeDtypeStruct((tok, width), BF),
             jax.ShapeDtypeStruct((tok, lanes), F32),
@@ -281,10 +344,10 @@
             u = u + gb2[o]
     else:
         u = lax.fori_loop(1, n, lambda o, u: u + gb2[o], hb[me])
-    ids = ids_ref[...]
+    ids = columns_of(ids_ref)
     top = ids.shape[1]
     mine = gg_ref.shape[1]
-    lane = lax.broadcasted_iota(jnp.int32, (rows, lanes), 1)
+    lane = lax.broadcasted_iota(jnp.int32, (rows, lanes), 1).astype(F32)
     spot = lax.broadcasted_iota(jnp.int32, (rows, mine), 1)
     res = jnp.zeros((rows, mine), F32)
     for k in range(top):
@@ -298,7 +361,7 @@
     lanes = dg.shape[1]
     rows = tok // n
     part = width // ndp
-    top = ids.shape[1]
+    top = ids.shape[0]
     dma = pltpu.SemaphoreType.DMA
     return pl.pallas_call(
         functools.partial(reduce_kernel, n, ndp),
@@ -330,12 +393,12 @@
     ndp = lax.axis_size("dp")
     exp_loc = w_gate.shape[1]
     lanes = -(-exp_loc * n // 128) * 128
-    xy, g = gather(tokens[0], out_grad[0], expert_ids[0], gates[0], n, ndp, lanes)
+    xy, g = gather(tokens[0], out_grad[0], expert_ids[0].T, gates[0].T, n, ndp, lanes)
     base = (lax.axis_index("expert") * exp_loc).astype(jnp.int32).reshape(1)
     dx, dg, dwg, dwu, dwd = experts(
         base, xy, g.reshape(-1, lanes), w_gate[0], w_up[0], w_down[0]
     )
-    prev, gg = reduce(dx, dg, expert_ids[0], n, ndp)
+    prev, gg = reduce(dx, dg, expert_ids[0].T, n, ndp)
     return prev.astype(BF)[None], gg[None], dwg[None], dwu[None], dwd[None]
 
 

time: 87.8 us -> 73.9 us (0.84)
  Pallas kernels: 81.4 us -> 70.3 us
  local copies, waits for them, and re-layouts: 4.03 us -> 1.33 us
    pallas_call x1, Pallas kernels: 49.5 us -> 38.3 us  [experts(): pl.pallas_call(functools.partial(expert_kernel, nin, nout), in_specs=[pl....]
    squeeze x2 -> x0, local copies, waits for them, and re-layouts: 2.7 us -> none  [the longest x1 1.35 us: local(): expert_ids[0]]
where the time goes in v2:
time: 73.9 us; the launch traced here: 73.6 us
  Pallas kernels  70.3 us (95%)
  other arithmetic  1.37 us (2%)
  local copies, waits for them, and re-layouts  1.33 us (2%)
    pallas_call x1, Pallas kernels, experts(): pl.pallas_call(functools.partial(expert_kernel, nin, nout), in_specs=[pl....  38.3 us
    pallas_call x1, Pallas kernels, gather(): pl.pallas_call(functools.partial(gather_kernel, n, ndp), out_shape=(jax.S...  16.1 us
    pallas_call x1, Pallas kernels, reduce(): pl.pallas_call(functools.partial(reduce_kernel, n, ndp), out_shape=(jax.S...  15.9 us

profile of v2, /device:TPU:0, one launch (start us, length us, event | category | flops | bytes accessed | tf_op | source)
XLA Modules:
  0.0 73.6 jit_solution(1909329832280277786)
XLA Ops:
  0.6 16.1 %gather_tokens.1 = (bf16[2,64,2048]{2,1,0:T(8,128)(2,1)}, f32[4,16,128]{2,1,0:T(8,128)}) custom-call(bf16[16,2048]{1,0:T(8,128)(2,1)} %bitcast.22, bf16[16,2048]{1,0:T(8,128)(2,1)} %bitcast.23, s32[8,16]{1,0:T(8,128)} %bitcast.25, bf16[8,16]{1,0:T(8,128)(2,1)} %bitcast.27), custom_call_target="tpu_custom_call" | custom-call | tf_op jit(solution)/shard_map/gather_tokens/pallas_call | solution.py:107
  16.7 38.3 %experts.1 = (bf16[64,2048]{1,0:T(8,128)(2,1)}, f32[64,128]{1,0:T(8,128)}, bf16[16,2048,256]{2,1,0:T(8,128)(2,1)}, bf16[16,2048,256]{2,1,0:T(8,128)(2,1)}, bf16[16,256,2048]{2,1,0:T(8,128)(2,1)}) custom-call(s32[1]{0:T(128)} %bitcast.base_ref, bf16[2,64,2048]{2,1,0:T(8,128)(2,1)} %get-tuple-element.14.xy_ref, f32[64,128]{1,0:T(8,128)} %bitcast.24, ...), custom_call_target="tpu_custom_call" | custom-call | tf_op jit(solution)/shard_map/experts/pallas_call | solution.py:246
  55.0 15.9 %reduce_dx.1 = (f32[16,512]{1,0:T(8,128)}, f32[16,2]{1,0:T(8,128)}) custom-call(bf16[64,2048]{1,0:T(8,128)(2,1)} %get-tuple-element.16.dx_ref, f32[64,128]{1,0:T(8,128)} %get-tuple-element.17.dg_ref, s32[8,16]{1,0:T(8,128)} %bitcast.26), custom_call_target="tpu_custom_call" | custom-call | tf_op jit(solution)/shard_map/reduce_dx/pallas_call | solution.py:366
  70.9 1.4 %convert_bitcast_fusion = bf16[1,16,512]{2,1,0:T(8,128)(2,1)} fusion(f32[16,512]{1,0:T(8,128)} %get-tuple-element.18), kind=kLoop, calls=%fused_computation | loop fusion | flops 8192 | bytes 49152 | tf_op jit(solution)/shard_map/broadcast_in_dim | solution.py:402
  72.3 1.3 %copy.12 = f32[16,2]{0,1:T(2,128)} copy(f32[16,2]{1,0:T(8,128)} %get-tuple-element.19) | data formatting | bytes 256 | tf_op jit(solution)/shard_map/reduce_dx/pallas_call | solution.py:366
